TPU v7x, 256 devices: a whole 4x4x8 slice. The times are simulated.
256 devices in a mesh: dp: 16 (over z, core), tensor: 16 (over x, y).
Axes of the slice: x: 4, y: 4, z: 8, core: 2. Of those that a mesh axis runs over, the one named last changes fastest.
Arguments:
- activations: bfloat16 [8192, 8192], P('dp'), may hold values from -6 to 6
- cotangent: bfloat16 [8192, 2048], P('dp', 'tensor')
- master_old: float32 [16, 16, 1032, 128], P('dp', 'tensor'), may hold values from -0.3125 to 0.3125
- first_old: float32 [16, 16, 1032, 128], P('dp', 'tensor'), may hold values from -6 to 6
- second_old: float32 [16, 16, 1032, 128], P('dp', 'tensor'), may hold values from 0.25 to 4
- old_lengths: int32 [12], replicated, may hold values from 1 to 1032, 8192 in all
- new_lengths: int32 [11], replicated, may hold values from 1 to 1120, 8192 in all
- failed: int32 [1], replicated, may hold values from 0 to 11
Outputs:
- master_new: float32 [16, 16, 1120, 128], P('dp', 'tensor')
- first_new: float32 [16, 16, 1120, 128], P('dp', 'tensor')
- second_new: float32 [16, 16, 1120, 128], P('dp', 'tensor')
- export_values: bfloat16 [16, 16, 1120, 128], P('dp', 'tensor')
- export_scales: float32 [16, 16, 4, 1120], P('dp', 'tensor')
Inputs may be any that keep to these rules, and one draw needn't show every extreme that they name: `old_lengths`: whole numbers of 1 or more that sum to 8192; the largest is 1032. `new_lengths`: whole numbers of 1 or more that sum to 8192; the largest is 1120.
All inputs are finite; a program needn't handle non-finite values.
Results may differ from a plain program's by a relative error of at most 0.001.
Values sent between devices are 32-bit elements; how exact they have to be, the bound alone decides.
A program may use at most 128 MiB of HBM per device.

v0:
```python
import jax
import jax.numpy as jnp
from jax import lax
from jax.sharding import PartitionSpec as P

beta_first = 0.9
beta_second = 0.95
learn_rate = 0.004
epsilon = 1e-08
scale_floor = 0.03


def offsets(lengths):
    return jnp.cumsum(lengths) - lengths


def lookup(table, index):
    slots = jnp.arange(table.shape[0], dtype=jnp.int32)
    return jnp.sum(jnp.where(index[..., None] == slots, table, 0), axis=-1)


def pack_pieces(arrays, src_start, src_len, dst_start, dst_len, slot):
    low_end = jnp.maximum(src_start, dst_start)
    high_end = jnp.minimum(src_start + src_len, dst_start + dst_len)
    offset_rows = jnp.arange(slot, dtype=jnp.int32)
    live = offset_rows[None, :] < (high_end - low_end)[:, None]
    result = []
    for array in arrays:
        source = jnp.clip(
            low_end[:, None] - src_start + offset_rows[None, :], 0, array.shape[0] - 1
        )
        result.append(jnp.where(live[..., None], array[source], jnp.zeros((), array.dtype)))
    return tuple(result)


def unpack_pieces(arrays, my_start, my_len, src_start, src_len, slot, capacity):
    position = jnp.arange(capacity, dtype=jnp.int32)
    target = my_start + position
    live = position < my_len
    inside = (target[:, None] >= src_start[None, :]) & (
        target[:, None] < (src_start + src_len)[None, :]
    )
    senders = jnp.arange(src_start.shape[0], dtype=jnp.int32)
    source = jnp.sum(jnp.where(inside, senders[None, :], 0), axis=1)
    base = jnp.sum(jnp.where(inside, src_start[None, :], 0), axis=1)
    base = jnp.maximum(base, my_start)
    index = jnp.clip(source * slot + target - base, 0, src_start.shape[0] * slot - 1)
    result = []
    for array in arrays:
        rows_flat = array.reshape(-1, array.shape[-1])
        result.append(jnp.where(live[:, None], rows_flat[index], jnp.zeros((), array.dtype)))
    return tuple(result)


def adam_step(master, first, second, grads):
    first = beta_first * first + (1.0 - beta_first) * grads
    second = beta_second * second + (1.0 - beta_second) * grads * grads
    correct_first = 1.0 - beta_first**10
    correct_second = 1.0 - beta_second**10
    master = master - learn_rate * (first / correct_first) / (
        jnp.sqrt(second / correct_second) + epsilon
    )
    return (master, first, second)


def export_blocks(master, live):
    blocks = master.reshape(master.shape[:-1] + (4, 32))
    largest = jnp.max(jnp.abs(blocks), axis=-1)
    scale = jnp.maximum(largest, scale_floor)
    values = (blocks / scale[..., None]).reshape(master.shape)
    values = jnp.where(live[..., None], values, 0.0).astype(jnp.bfloat16)
    scales = jnp.where(live[..., None], scale, 0.0)
    return (values, jnp.swapaxes(scales, -1, -2))


def on_device(
    activations, cotangent, master_old, first_old, second_old, old_lengths, new_lengths, failed
):
    dp_count = lax.axis_size("dp")
    tensor_count = lax.axis_size("tensor")
    my_index = lax.axis_index("dp")
    old_groups = old_lengths.shape[0]
    new_groups = new_lengths.shape[0]
    features = activations.shape[1]
    width = cotangent.shape[1]
    block_count = width // 128
    rows_all = features * width // 128
    cap_old = master_old.shape[2]
    cap_new = (rows_all * 3 // (2 * new_groups) // 8 + 1) * 8
    half_count = dp_count // 2
    devices = jnp.arange(dp_count, dtype=jnp.int32)
    lost = failed[0]
    old_len_pad = jnp.concatenate([old_lengths, jnp.zeros((dp_count - old_groups,), jnp.int32)])
    old_start_pad = offsets(old_len_pad)
    lost_len = lookup(old_len_pad, lost)
    lost_start = lookup(old_start_pad, lost)
    old_len_dev = jnp.where(
        devices == lost, 0, jnp.where(devices == old_groups, lost_len, old_len_pad)
    )
    old_start_dev = jnp.where(
        devices == old_groups, lost_start, jnp.where(devices == lost, 0, old_start_pad)
    )
    shifted = (devices + dp_count - half_count) % dp_count
    group = shifted - (shifted > lost).astype(jnp.int32)
    valid = (shifted != lost) & (group < new_groups)
    group = jnp.clip(group, 0, new_groups - 1)
    new_start = offsets(new_lengths)
    dst_start = jnp.where(valid, lookup(new_start, group), 0)
    dst_len = jnp.where(valid, lookup(new_lengths, group), 0)
    my_start = lookup(dst_start, my_index)
    my_len = lookup(dst_len, my_index)

    def grad_window(first_row, count, live):
        window = min(count // block_count + 2, features)
        first_feature = jnp.clip(first_row // block_count, 0, features - window)
        columns = lax.dynamic_slice_in_dim(activations, first_feature, window, 1)
        product = jnp.einsum("tc,tk->ck", columns, cotangent, preferred_element_type=jnp.float32)
        padded = jnp.concatenate([product, jnp.zeros((count, 128), jnp.float32)], axis=0)
        offset_rows = first_row - first_feature * block_count
        picked = lax.dynamic_slice_in_dim(padded, offset_rows, count, 0)
        return jnp.where(live[:, None], picked, 0.0)

    holders = jnp.arange(lax.axis_size("dp") * cap_new // cap_new, dtype=jnp.int32)

    def one_holder(holder):
        position = jnp.arange(cap_new, dtype=jnp.int32)
        return grad_window(lookup(dst_start, holder), cap_new, position < lookup(dst_len, holder))

    grads = lax.psum_scatter(
        lax.map(one_holder, holders).reshape(lax.axis_size("dp") * cap_new, 128),
        "dp",
        scatter_dimension=0,
        tiled=True,
    )
    squares = jnp.sum(grads * grads)
    total = lax.psum(squares, ("dp", "tensor"))
    count_all = float(features * width * tensor_count)
    clip = 1.0 / jnp.maximum(jnp.sqrt(total / count_all), 1.0)
    owned = (master_old[0, 0], first_old[0, 0], second_old[0, 0])
    my_old_start = lookup(old_start_dev, my_index)
    my_old_len = lookup(old_len_dev, my_index)
    slot = min(cap_old, cap_new)
    outgoing_state = pack_pieces(owned, my_old_start, my_old_len, dst_start, dst_len, slot)
    received = (
        lax.all_to_all(outgoing_state[0], "dp", split_axis=0, concat_axis=0, tiled=True),
        lax.all_to_all(outgoing_state[1], "dp", split_axis=0, concat_axis=0, tiled=True),
        lax.all_to_all(outgoing_state[2], "dp", split_axis=0, concat_axis=0, tiled=True),
    )
    master, first, second = unpack_pieces(
        received, my_start, my_len, old_start_dev, old_len_dev, slot, cap_new
    )
    master, first, second = adam_step(master, first, second, clip * grads)
    live = jnp.arange(cap_new, dtype=jnp.int32) < my_len
    values, scales = export_blocks(master, live)
    return (
        master[None, None],
        first[None, None],
        second[None, None],
        values[None, None],
        scales[None, None],
    )


def solution(mesh):
    placed = (
        P("dp", None),
        P("dp", "tensor"),
        P("dp", "tensor", None, None),
        P("dp", "tensor", None, None),
        P("dp", "tensor", None, None),
        P(),
        P(),
        P(),
    )
    return jax.shard_map(
        on_device,
        mesh=mesh,
        in_specs=placed,
        out_specs=(
            P("dp", "tensor", None, None),
            P("dp", "tensor", None, None),
            P("dp", "tensor", None, None),
            P("dp", "tensor", None, None),
            P("dp", "tensor", None, None),
        ),
        check_vma=False,
    )
```

profile of v0, /device:TPU:1, one launch (start us, length us, event | category | flops | bytes accessed | tf_op | source)
XLA Modules:
  0.0 840.1 jit_solution(7494594890363757131)
XLA Ops:
  17.9 31.2 %gather_fusion.2 = f32[16512,128]{1,0:T(8,128)} fusion(f32[1032,128]{1,0:T(8,128)S(1)} %bitcast.49, s32[17408]{0:T(1024)S(1)} %pad_clamp_fusion), kind=kCustom, calls=%fused_computation.2 | custom fusion | bytes 16974336 | tf_op jit(solution)/shard_map/gather | solution.py:32
  49.0 31.1 %gather_fusion.4 = f32[16512,128]{1,0:T(8,128)} fusion(f32[1032,128]{1,0:T(8,128)S(1)} %bitcast.50, s32[17408]{0:T(1024)S(1)} %pad_clamp_fusion), kind=kCustom, calls=%fused_computation.4 | custom fusion | bytes 16974336 | tf_op jit(solution)/shard_map/gather | solution.py:32
  80.2 31.1 %gather_fusion = f32[16512,128]{1,0:T(8,128)} fusion(f32[1032,128]{1,0:T(8,128)S(1)} %bitcast.51, s32[17408]{0:T(1024)S(1)} %pad_clamp_fusion), kind=kCustom, calls=%fused_computation | custom fusion | bytes 16974336 | tf_op jit(solution)/shard_map/gather | solution.py:32
  111.4 18.6 %broadcast_select_fusion.2 = (f32[16,1032,128]{2,1,0:T(8,128)}, f32[16,1032,128]{2,1,0:T(8,128)}, f32[16,1032,128]{2,1,0:T(8,128)}) fusion(f32[16,1032,128]{2,1,0:T(8,128)} %bitcast.54, pred[16,1032]{1,0:T(8,128)(4,1)S(1)} %iota_compare_fusion.1, f32[16,1032,128]{2,1,0:T(8,128)} %bitcast.52, f32[16,1032,128]{2,1,0:T(8,128)} %bitcast.53), kind=kLoop, calls=%fused_computation.20 | loop fusion | flops 6340608 | bytes 50741376 | tf_op jit(solution)/shard_map/jit(_where)/select_n | solution.py:32
  130.0 10.0 %all-to-all-start = ((f32[16,1032,128]{2,1,0:T(8,128)}), f32[16,1032,128]{2,1,0:T(8,128)}, u32[]{:S(2)}, u32[]{:S(2)}) async-start(f32[16,1032,128]{2,1,0:T(8,128)} %get-tuple-element.132), calls=%async_computation | async-start | bytes 16908288 | tf_op jit(solution)/shard_map/all_to_all | solution.py:145
  140.0 184.9 %all-to-all-done = f32[16,1032,128]{2,1,0:T(8,128)} async-done(((f32[16,1032,128]{2,1,0:T(8,128)}), f32[16,1032,128]{2,1,0:T(8,128)}, u32[]{:S(2)}, u32[]{:S(2)}) %all-to-all-start) | async-done | bytes 8454176 | tf_op jit(solution)/shard_map/all_to_all | solution.py:145
  324.9 5.7 all-to-all-start.1
  330.6 113.0 %while.12 = (s32[]{:T(128)}, f32[16,1120,128]{2,1,0:T(8,128)}, s32[16]{0:T(128)S(1)}, s32[16]{0:T(128)S(1)}, s32[16]{0:T(128)S(1)}, /*index=5*/bf16[512,8192]{1,...) while((s32[]{:T(128)}, f32[16,1120,128]{2,1,0:T(8,128)}, ...), condition=%wide.region_15.16_spmd, body=%wide.region_12.15_spmd.sunk | while | flops 147207344 | bytes 3036183 | solution.py:130
  333.7 2.3 fusion.29
  340.7 2.3 fusion.29
  354.8 2.3 fusion.29
  361.8 2.3 fusion.29
  368.9 2.3 fusion.29
  376.0 2.3 fusion.29
  383.0 2.3 fusion.29
  390.1 2.3 fusion.29
  397.2 2.3 fusion.29
  404.2 2.3 fusion.29
  411.3 2.3 fusion.29
  418.4 2.3 fusion.29
  425.4 2.3 fusion.29
  432.5 2.3 fusion.29
  439.6 2.3 fusion.29
  443.7 86.0 %all-to-all-done.1 = f32[16,1032,128]{2,1,0:T(8,128)} async-done(((f32[16,1032,128]{2,1,0:T(8,128)}), f32[16,1032,128]{2,1,0:T(8,128)}, u32[]{:S(2)}, u32[]{:S(2)}) %all-to-all-start.1) | async-done | bytes 8454176 | tf_op jit(solution)/shard_map/all_to_all | solution.py:146
  529.7 6.3 all-to-all-start.2
  538.8 5.9 gather_fusion.1
  544.7 5.9 gather_fusion.3
  550.6 162.5 %reduce-scatter.2.cloned.1.call-done = f32[1120,128]{1,0:T(8,128)} async-done(((f32[17920,128]{1,0:T(8,128)}), f32[1120,128]{1,0:T(8,128)}) %reduce-scatter.2.cloned.1.call-update) | async-done | bytes 573456 | tf_op jit(solution)/shard_map/reduce_scatter | solution.py:129
  714.9 30.8 %all-to-all-done.2 = f32[16,1032,128]{2,1,0:T(8,128)} async-done(((f32[16,1032,128]{2,1,0:T(8,128)}), f32[16,1032,128]{2,1,0:T(8,128)}, u32[]{:S(2)}, u32[]{:S(2)}) %all-to-all-start.2) | async-done | bytes 8454176 | tf_op jit(solution)/shard_map/all_to_all | solution.py:147
  745.7 5.8 gather_fusion.5
  751.5 76.3 %psum.7 = f32[]{:T(128)} all-reduce(f32[]{:T(128)} %multiply_reduce_fusion), channel_id=1, replica_groups=mesh['dp'=16,'tensor'=16] {'dp','tensor'}, use_global_device_ids=true, to_apply=%region_18.19 | all-reduce | flops 1 | bytes 8 | tf_op jit(solution)/shard_map/psum | solution.py:136
  828.5 2.6 fusion.18
  (112 shorter events, 75.2 us)
Async XLA Ops:
  7.2 10.7 %copy-start = (f32[1,1,1032,128]{3,2,1,0:T(8,128)S(1)}, f32[1,1,1032,128]{3,2,1,0:T(8,128)}, u32[]{:S(2)}) copy-start(f32[1,1,1032,128]{3,2,1,0:T(8,128)} %param.13) | copy-start | bytes 1585156
  17.9 31.2 %copy-start.2 = (f32[1,1,1032,128]{3,2,1,0:T(8,128)S(1)}, f32[1,1,1032,128]{3,2,1,0:T(8,128)}, u32[]{:S(2)}) copy-start(f32[1,1,1032,128]{3,2,1,0:T(8,128)} %param.14) | copy-start | bytes 1585156
  49.0 31.1 %copy-start.3 = (f32[1,1,1032,128]{3,2,1,0:T(8,128)S(1)}, f32[1,1,1032,128]{3,2,1,0:T(8,128)}, u32[]{:S(2)}) copy-start(f32[1,1,1032,128]{3,2,1,0:T(8,128)} %param.12) | copy-start | bytes 1585156
  130.0 194.8 %all-to-all-start = ((f32[16,1032,128]{2,1,0:T(8,128)}), f32[16,1032,128]{2,1,0:T(8,128)}, u32[]{:S(2)}, u32[]{:S(2)}) async-start(f32[16,1032,128]{2,1,0:T(8,128)} %get-tuple-element.132), calls=%async_computation | async-start | bytes 16908288 | tf_op jit(solution)/shard_map/all_to_all | solution.py:145
  324.9 5.8 copy-start.4
  324.9 204.9 %all-to-all-start.1 = ((f32[16,1032,128]{2,1,0:T(8,128)}), f32[16,1032,128]{2,1,0:T(8,128)}, u32[]{:S(2)}, u32[]{:S(2)}) async-start(f32[16,1032,128]{2,1,0:T(8,128)} %get-tuple-element.133), calls=%async_computation.1 | async-start | bytes 16908288 | tf_op jit(solution)/shard_map/all_to_all | solution.py:146
  330.6 382.5 %reduce-scatter.2.cloned.1.call-start = ((), (), s32[]{:S(2)}) async-start(), calls=%async_computation.4 | async-start | bytes 9748480 | tf_op jit(solution)/shard_map/reduce_scatter | solution.py:129
  529.7 215.9 %all-to-all-start.2 = ((f32[16,1032,128]{2,1,0:T(8,128)}), f32[16,1032,128]{2,1,0:T(8,128)}, u32[]{:S(2)}, u32[]{:S(2)}) async-start(f32[16,1032,128]{2,1,0:T(8,128)} %get-tuple-element.134), calls=%async_computation.3 | async-start | bytes 16908288 | tf_op jit(solution)/shard_map/all_to_all | solution.py:147
  544.7 288.6 %copy-start.1 = (f32[1,1,1032,128]{3,2,1,0:T(8,128)S(1)}, f32[1,1,1032,128]{3,2,1,0:T(8,128)}, u32[]{:S(2)}) copy-start(f32[1,1,1032,128]{3,2,1,0:T(8,128)} %param.13) | copy-start | bytes 1585156
  831.1 2.1 copy-start.5
Sparse Core Ops, SparseCore 0:
  443.8 269.2 reduce-scatter.1
where the time goes:
time: 842 us; the launch traced here: 840 us
  waiting for transfers between devices  464 us (55%)
  local copies, waits for them, and re-layouts  122 us (14%)
  other arithmetic  83.5 us (10%)
  blocking collectives  76.3 us (9%)
  matrix products  36.7 us (4%)
  starting transfers between devices  22 us (3%)
  loops' own time  18.8 us (2%)
  between operations  16.9 us (2%)
    all_to_all x1, waiting for transfers between devices, on_device(): lax.all_to_all(outgoing_state[0], 'dp', split_axis=0, concat_axis=0, tile...  185 us
    reduce_scatter x1, waiting for transfers between devices, on_device(): lax.psum_scatter(lax.map(one_holder, holders).reshape(lax.axis_size('dp')...  162 us
    gather x3, local copies, waits for them, and re-layouts, pack_pieces(): array[source]  93.4 us
    all_to_all x1, waiting for transfers between devices, on_device(): lax.all_to_all(outgoing_state[1], 'dp', split_axis=0, concat_axis=0, tile...  86 us
    psum x1, blocking collectives, on_device(): total = lax.psum(squares, ('dp', 'tensor'))  76.3 us
    dot_general x16, matrix products, grad_window(): jnp.einsum('tc,tk->ck', columns, cotangent, preferred_element_type=jnp.fl...  36.7 us
    all_to_all x1, waiting for transfers between devices, on_device(): lax.all_to_all(outgoing_state[2], 'dp', split_axis=0, concat_axis=0, tile...  30.8 us
    reduce_sum x20, other arithmetic, lookup(): return jnp.sum(jnp.where(index[..., None] == slots, table, 0), axis=-1)  24 us
  transfers between devices with their start and end apart: 4, of which 4 were waited for; matrix products, arithmetic and copies ran while one was open for 13% of the time, Pallas kernels for 0%

commit v1 on v0

v1 whole, which is shorter than its diff:
```python
import functools

import jax
import jax.numpy as jnp
from jax import lax
from jax.experimental import pallas as pl
from jax.experimental.pallas import tpu as pltpu
from jax.sharding import PartitionSpec as P

MESH = pl.DeviceIdType.MESH
beta_first = 0.9
beta_second = 0.95
learn_rate = 0.004
epsilon = 1e-08
scale_floor = 0.03

DP = 16
CHIPS = 8
OLD_GROUPS = 12
NEW_GROUPS = 11
FEATURES = 8192
TOKENS = 512
CAP_OLD = 1032
CAP_NEW = 1120
MID = 512
HALF = MID // 2
OLD_BLOCKS = 66
NEW_BLOCKS = 71
SLOT_OLD = 200
SLOT_NEW = 216
LAND = SLOT_OLD + 8
FEATURE_BLOCK = 512
F32 = jnp.float32

STREAMS = ((1, 0, 4), (-1, 1, 4), (1, 1, 3), (-1, 0, 3))
STREAM_BASE = (0, 4, 8, 11)


def prefix(ref, count):
    starts, at = [], jnp.int32(0)
    for i in range(count):
        starts.append(at)
        at = at + ref[i]
    return starts


def pick(index, values):
    result = values[0]
    for i in range(1, len(values)):
        result = jnp.where(index == i, values[i], result)
    return result


def new_group(holder, lost):
    return holder - jnp.where(holder > lost, 1, 0)


def exchange(
    act_hbm, cot_ref, master_hbm, first_hbm, second_hbm, old_ref, new_ref, lost_ref,
    out_hbm,
    act, cot_t, prod, state, send_old, land_old, sib_send, sib_land, ring_send, ring_land,
    grads, squares, squares_dp, squares_tensor, middle, send_new, starts,
    act_sem, state_sem, local_sem, old_ssem, old_rsem, sib_ssem, sib_rsem, ring_ssem, ring_rsem,
    sq_ssem, sq_rsem, new_ssem, new_rsem,
):
    dp = lax.axis_index("dp")
    tensor = lax.axis_index("tensor")
    chip = lax.div(dp, 2)
    core = lax.rem(dp, 2)
    lost = lost_ref[0]

    def remote(src, dst, ssem, rsem, to_dp, to_tensor=None):
        return pltpu.make_async_remote_copy(
            src_ref=src, dst_ref=dst, send_sem=ssem, recv_sem=rsem,
            device_id=(to_dp, tensor if to_tensor is None else to_tensor),
            device_id_type=MESH,
        )

    barrier = pltpu.get_barrier_semaphore()
    for d in range(1, DP):
        pl.semaphore_signal(
            barrier, inc=1, device_id=(lax.rem(dp + d, DP), tensor), device_id_type=MESH
        )
        pl.semaphore_signal(
            barrier, inc=1, device_id=(dp, lax.rem(tensor + d, DP)), device_id_type=MESH
        )

    state_in = [
        pltpu.make_async_copy(src, state.at[a, pl.ds(16, CAP_OLD)], state_sem.at[a])
        for a, src in enumerate((master_hbm, first_hbm, second_hbm))
    ]
    for copy in state_in:
        copy.start()
    blocks = FEATURES // FEATURE_BLOCK
    act_in = []
    for b in range(blocks):
        columns = pl.ds(b * FEATURE_BLOCK, FEATURE_BLOCK)
        act_in.append(
            pltpu.make_async_copy(act_hbm.at[:, columns], act.at[:, columns], act_sem.at[b])
        )
        act_in[-1].start()

    old_start = prefix(old_ref, OLD_GROUPS)
    new_start = prefix(new_ref, NEW_GROUPS)
    my_group = jnp.where(dp == OLD_GROUPS, lost, dp)
    my_old = pick(my_group, old_start)
    shift = 16 - lax.rem(my_old, 16)
    for h in range(OLD_GROUPS):
        g = jnp.clip(new_group(jnp.int32(h), lost), 0, NEW_GROUPS - 1)
        starts[(h + DP // 2) % DP] = pick(g, new_start)

    for copy in state_in:
        copy.wait()
    pl.semaphore_wait(barrier, 2 * (DP - 1))

    def pack_old(dst, put):
        for a in range(3):
            put(a, state[a, pl.ds(shift + dst, OLD_BLOCKS, stride=16), :])

    old_copies = []
    for d in range(1, DP):
        dst = lax.rem(dp + d, DP)
        old_copies.append(
            remote(
                send_old.at[d], land_old.at[pl.ds(dp * LAND + 8, SLOT_OLD)],
                old_ssem.at[d], old_rsem.at[d], dst,
            )
        )

    @pl.when(dp <= OLD_GROUPS)
    def _():
        for d in (8, 9, 7, 10, 6, 11, 5, 12, 4, 13, 3, 14, 2, 15, 1):
            def put(a, rows):
                send_old[d, pl.ds(a * OLD_BLOCKS, OLD_BLOCKS), :] = rows

            pack_old(lax.rem(dp + d, DP), put)
            old_copies[d - 1].start()

        def put_own(a, rows):
            land_old[pl.ds(dp * LAND + 8 + a * OLD_BLOCKS, OLD_BLOCKS), :] = rows

        pack_old(dp, put_own)

    cot_t[...] = cot_ref[...].T
    for b in range(blocks):
        act_in[b].wait()

    def multiply(b, carry):
        columns = pl.ds(pl.multiple_of(b * FEATURE_BLOCK, FEATURE_BLOCK), FEATURE_BLOCK)
        turned = jnp.dot(cot_t[...], act[:, columns], preferred_element_type=F32)
        prod[columns, :] = turned.T
        return carry

    lax.fori_loop(0, blocks, multiply, 0)

    sibling = dp + 1 - 2 * core
    sib_copies = {}
    for off in (4, 3, 5, 2, 6, 1, 7, 0):
        c = lax.rem(chip + off, CHIPS) * 2 + 1 - core
        sib_send[off] = prod[pl.ds(c, MID, stride=16), :]
        sib_copies[off] = remote(
            sib_send.at[off], sib_land.at[off], sib_ssem.at[off], sib_rsem.at[off], sibling
        )
        sib_copies[off].start()

    arrived = set()

    def partial(off, half):
        off = off % CHIPS
        if off not in arrived:
            sib_copies[off].wait_recv()
            arrived.add(off)
        c = lax.rem(chip + off, CHIPS) * 2 + core
        own = prod[pl.ds(c + 16 * HALF * half, HALF, stride=16), :]
        return own + sib_land[off, pl.ds(HALF * half, HALF), :]

    ring_copies = {}
    for k in range(1, 5):
        for s, (way, half, hops) in enumerate(STREAMS):
            if k > hops:
                continue
            n = STREAM_BASE[s] + k - 1
            total = partial(way * (hops + 1 - k), half)
            if k > 1:
                ring_copies[n - 1].wait_recv()
                total = total + ring_land[n - 1]
            ring_send[n] = total
            neighbour = lax.rem(chip + way + CHIPS, CHIPS) * 2 + core
            ring_copies[n] = remote(
                ring_send.at[n], ring_land.at[n], ring_ssem.at[n], ring_rsem.at[n], neighbour
            )
            ring_copies[n].start()
    ends = [STREAM_BASE[s] + STREAMS[s][2] - 1 for s in range(4)]
    for n in ends:
        ring_copies[n].wait_recv()
    square = jnp.zeros((8, 128), F32)
    for half in range(2):
        total = partial(0, half)
        for s in range(4):
            if STREAMS[s][1] == half:
                total = total + ring_land[ends[s]]
        grads[pl.ds(HALF * half, HALF), :] = total
        square = square + jnp.sum((total * total).reshape(HALF // 8, 8, 128), axis=0)

    def gather(mine, land, base, axis_dp):
        copies = []
        for d in range(1, DP):
            to_dp = lax.rem(dp + d, DP) if axis_dp else dp
            to_tensor = tensor if axis_dp else lax.rem(tensor + d, DP)
            copies.append(
                remote(
                    mine, land.at[d], sq_ssem.at[base + d], sq_rsem.at[base + d], to_dp, to_tensor
                )
            )
            copies[-1].start()
        return copies

    squares[0] = square
    first_gather = gather(squares.at[0], squares_dp, 0, True)
    for copy in first_gather:
        copy.wait_recv()
    for d in range(1, DP):
        square = square + squares_dp[d]
    squares[1] = square
    second_gather = gather(squares.at[1], squares_tensor, DP, False)
    for copy in second_gather:
        copy.wait_recv()
    for d in range(1, DP):
        square = square + squares_tensor[d]
    total = jnp.sum(jnp.sum(square, axis=1, keepdims=True), axis=0, keepdims=True)
    count_all = float(FEATURES * 128 * DP)
    clip = 1.0 / jnp.maximum(jnp.sqrt(total / count_all), 1.0)

    for d in range(1, DP):
        @pl.when(lax.rem(dp - d + DP, DP) <= OLD_GROUPS)
        def _():
            old_copies[d - 1].wait_recv()

    correct_first = 1.0 - beta_first**10
    correct_second = 1.0 - beta_second**10
    slots = [jnp.where(lost == i, OLD_GROUPS, i) * LAND + 8 for i in range(OLD_GROUPS)]
    old_block = [lax.div(s, 16) for s in old_start]
    old_end = [old_start[i] + old_ref[i] for i in range(OLD_GROUPS)]

    def update(m, carry):
        base = pl.multiple_of(m * 8, 8)
        row = 16 * (base + lax.broadcasted_iota(jnp.int32, (8, 128), 0)) + dp
        values = [jnp.zeros((8, 128), F32) for _ in range(3)]
        for i in range(OLD_GROUPS):
            live = (row >= old_start[i]) & (row < old_end[i])
            at = slots[i] + jnp.clip(base - old_block[i], -8, OLD_BLOCKS)
            for a in range(3):
                rows = land_old[pl.ds(at + a * OLD_BLOCKS, 8), :]
                values[a] = jnp.where(live, rows, values[a])
        master, first, second = values
        g = clip * grads[pl.ds(base, 8), :]
        first = beta_first * first + (1.0 - beta_first) * g
        second = beta_second * second + (1.0 - beta_second) * g * g
        master = master - learn_rate * (first / correct_first) / (
            jnp.sqrt(second / correct_second) + epsilon
        )
        middle[0, pl.ds(base, 8), :] = master
        middle[1, pl.ds(base, 8), :] = first
        middle[2, pl.ds(base, 8), :] = second
        return carry

    lax.fori_loop(0, MID // 8, update, 0)

    def holds(device):
        return (device >= DP // 2) | (device < DP // 2 + OLD_GROUPS - DP)

    new_copies = []
    for d in range(DP):
        dst = lax.rem(dp + d, DP)
        if d:
            copy = remote(
                send_new.at[d], out_hbm.at[dp], new_ssem.at[d], new_rsem.at[d], dst
            )
        else:
            copy = pltpu.make_async_copy(send_new.at[0], out_hbm.at[dp], local_sem)
        new_copies.append(copy)
    for d in (8, 9, 7, 10, 6, 11, 5, 12, 4, 13, 3, 14, 2, 15, 1, 0):
        dst = lax.rem(dp + d, DP)

        @pl.when(holds(dst))
        def _():
            at = lax.div(starts[dst], 16)
            for a in range(3):
                send_new[d, pl.ds(a * NEW_BLOCKS, NEW_BLOCKS), :] = middle[
                    a, pl.ds(at, NEW_BLOCKS), :
                ]
            new_copies[d].start()

    @pl.when(holds(dp))
    def _():
        for d in range(1, DP):
            new_copies[d].wait_recv()
        new_copies[0].wait()

    for d in range(1, DP):
        @pl.when(holds(lax.rem(dp + d, DP)))
        def _():
            new_copies[d].wait_send()

    @pl.when(dp <= OLD_GROUPS)
    def _():
        for copy in old_copies:
            copy.wait_send()

    for copy in list(sib_copies.values()) + list(ring_copies.values()):
        copy.wait_send()
    for copy in first_gather + second_gather:
        copy.wait_send()


def place(
    land, new_ref, lost_ref, master_ref, first_ref, second_ref, values_ref, scales_ref, rows
):
    dp = lax.axis_index("dp")
    lost = lost_ref[0]
    new_start = prefix(new_ref, NEW_GROUPS)
    holder = lax.rem(dp + DP // 2, DP)
    group = jnp.clip(new_group(holder, lost), 0, NEW_GROUPS - 1)
    held = (holder != lost) & (holder < OLD_GROUPS)
    start = pick(group, new_start)
    length = jnp.where(held, pick(group, [new_ref[i] for i in range(NEW_GROUPS)]), 0)
    for a in range(3):
        for c in range(DP):
            rows[a, pl.ds(c, NEW_BLOCKS, stride=16), :] = land[
                c, pl.ds(a * NEW_BLOCKS, NEW_BLOCKS), :
            ]
    offset = lax.rem(start, 16)
    step = 128
    for at in range(0, CAP_NEW, step):
        size = min(step, CAP_NEW - at)
        live = at + lax.broadcasted_iota(jnp.int32, (size, 128), 0) < length
        taken = [
            jnp.where(live, rows[a, pl.ds(offset + at, size), :], 0.0) for a in range(3)
        ]
        master_ref[pl.ds(at, size), :] = taken[0]
        first_ref[pl.ds(at, size), :] = taken[1]
        second_ref[pl.ds(at, size), :] = taken[2]
        turned = taken[0].T
        live_turned = at + lax.broadcasted_iota(jnp.int32, (1, size), 1) < length
        parts = []
        for b in range(4):
            block = turned[32 * b : 32 * b + 32]
            scale = jnp.maximum(jnp.max(jnp.abs(block), axis=0, keepdims=True), scale_floor)
            parts.append(block / scale)
            scales_ref[pl.ds(b, 1), pl.ds(at, size)] = jnp.where(live_turned, scale, 0.0)
        values_ref[pl.ds(at, size), :] = jnp.concatenate(parts, axis=0).T.astype(jnp.bfloat16)


def on_device(
    activations, cotangent, master_old, first_old, second_old, old_lengths, new_lengths, failed
):
    vmem = pl.BlockSpec(memory_space=pltpu.VMEM)
    smem = pl.BlockSpec(memory_space=pltpu.SMEM)
    anywhere = pl.BlockSpec(memory_space=pl.ANY)
    dma = pltpu.SemaphoreType.DMA
    landed = pl.pallas_call(
        exchange,
        out_shape=jax.ShapeDtypeStruct((DP, SLOT_NEW, 128), F32),
        in_specs=[anywhere, vmem, anywhere, anywhere, anywhere, smem, smem, smem],
        out_specs=anywhere,
        scratch_shapes=[
            pltpu.VMEM((TOKENS, FEATURES), jnp.bfloat16),
            pltpu.VMEM((128, TOKENS), jnp.bfloat16),
            pltpu.VMEM((FEATURES, 128), F32),
            pltpu.VMEM((3, CAP_OLD + 56, 128), F32),
            pltpu.VMEM((DP, SLOT_OLD, 128), F32),
            pltpu.VMEM((DP * LAND, 128), F32),
            pltpu.VMEM((CHIPS, MID, 128), F32),
            pltpu.VMEM((CHIPS, MID, 128), F32),
            pltpu.VMEM((14, HALF, 128), F32),
            pltpu.VMEM((14, HALF, 128), F32),
            pltpu.VMEM((MID, 128), F32),
            pltpu.VMEM((2, 8, 128), F32),
            pltpu.VMEM((DP, 8, 128), F32),
            pltpu.VMEM((DP, 8, 128), F32),
            pltpu.VMEM((3, MID + 80, 128), F32),
            pltpu.VMEM((DP, SLOT_NEW, 128), F32),
            pltpu.SMEM((DP,), jnp.int32),
            dma((FEATURES // FEATURE_BLOCK,)),
            dma((3,)),
            dma,
            dma((DP,)),
            dma((DP,)),
            dma((CHIPS,)),
            dma((CHIPS,)),
            dma((14,)),
            dma((14,)),
            dma((2 * DP,)),
            dma((2 * DP,)),
            dma((DP,)),
            dma((DP,)),
        ],
        compiler_params=pltpu.CompilerParams(
            collective_id=0, has_side_effects=True, vmem_limit_bytes=56 * 2**20
        ),
    )(
        activations,
        cotangent,
        master_old[0, 0],
        first_old[0, 0],
        second_old[0, 0],
        old_lengths,
        new_lengths,
        failed,
    )
    wide = jax.ShapeDtypeStruct((CAP_NEW, 128), F32)
    outs = pl.pallas_call(
        place,
        out_shape=(
            wide,
            wide,
            wide,
            jax.ShapeDtypeStruct((CAP_NEW, 128), jnp.bfloat16),
            jax.ShapeDtypeStruct((4, CAP_NEW), F32),
        ),
        in_specs=[vmem, smem, smem],
        out_specs=(vmem,) * 5,
        scratch_shapes=[pltpu.VMEM((3, NEW_BLOCKS * 16 + 16, 128), F32)],
        compiler_params=pltpu.CompilerParams(vmem_limit_bytes=32 * 2**20),
    )(landed, new_lengths, failed)
    return tuple(out[None, None] for out in outs)


def solution(mesh):
    held = P("dp", "tensor", None, None)
    return jax.shard_map(
        on_device,
        mesh=mesh,
        in_specs=(P("dp", None), P("dp", "tensor"), held, held, held, P(), P(), P()),
        out_specs=(held,) * 5,
        check_vma=False,
    )
```

time: 842 us -> 130 us (0.15)
  waiting for transfers between devices: 464 us -> 0 us
  Pallas kernels: 0 us -> 127 us
  local copies, waits for them, and re-layouts: 122 us -> 1.47 us
  other arithmetic: 83.5 us -> 0 us
  blocking collectives: 76.3 us -> 0 us
  matrix products: 36.7 us -> 0 us
  starting transfers between devices: 22 us -> 0 us
  loops' own time: 18.8 us -> 0 us
  between operations: 16.9 us -> 1.33 us
    all_to_all x3 -> x0, waiting for transfers between devices: 302 us -> none  [the longest x1 185 us: on_device(): lax.all_to_all(outgoing_state[0], 'dp', split_axis=0, concat_axis=0, tile...]
    reduce_scatter x1 -> x0, waiting for transfers between devices: 162 us -> none  [on_device(): lax.psum_scatter(lax.map(one_holder, holders).reshape(lax.axis_size('dp')...]
    pallas_call x0 -> x2, Pallas kernels: none -> 127 us  [the longest x1 124 us: on_device(): pl.pallas_call(exchange, out_shape=jax.ShapeDtypeStruct((DP, SLOT_NEW, 12...]
    gather x6 -> x0, local copies, waits for them, and re-layouts: 111 us -> none  [the longest x3 93.4 us: pack_pieces(): array[source]]
    psum x1 -> x0, blocking collectives: 76.3 us -> none  [on_device(): total = lax.psum(squares, ('dp', 'tensor'))]
    dot_general x16 -> x0, matrix products: 36.7 us -> none  [grad_window(): jnp.einsum('tc,tk->ck', columns, cotangent, preferred_element_type=jnp.fl...]
    reduce_sum x22 -> x0, other arithmetic: 25.9 us -> none  [the longest x20 24 us: lookup(): return jnp.sum(jnp.where(index[..., None] == slots, table, 0), axis=-1)]
    all_to_all x3 -> x0, starting transfers between devices: 22 us -> none  [the longest x1 9.98 us: on_device(): lax.all_to_all(outgoing_state[0], 'dp', split_axis=0, concat_axis=0, tile...]
  transfers between devices with their start and end apart: 4 -> 0, of which waited for: 4 -> 0; matrix products, arithmetic and copies ran while one was open for 13% -> 0% of each run, Pallas kernels for 0% -> 0%
where the time goes in v1:
time: 130 us
  Pallas kernels  127 us (98%)
  local copies, waits for them, and re-layouts  1.47 us (1%)
  between operations  1.33 us (1%)
    pallas_call x1, Pallas kernels, on_device(): pl.pallas_call(exchange, out_shape=jax.ShapeDtypeStruct((DP, SLOT_NEW, 12...  124 us
    pallas_call x1, Pallas kernels, on_device(): pl.pallas_call(place, out_shape=(wide, wide, wide, jax.ShapeDtypeStruct((...  2.98 us

profile of v1, /device:TPU:1, one launch (start us, length us, event | category | flops | bytes accessed | tf_op | source)
XLA Modules:
  0.0 130.2 jit_solution(7350123189255268799)
XLA Ops:
  0.6 0.0 copy-start.1
  1.3 124.4 %shard_map.119.land = f32[16,216,128]{2,1,0:T(8,128)} custom-call(bf16[512,8192]{1,0:T(8,128)(2,1)} %act_hbm.1, bf16[512,128]{1,0:T(8,128)(2,1)} %cot_ref.1, f32[1032,128]{1,0:T(8,128)} %bitcast.8, f32[1032,128]{1,0:T(8,128)} %bitcast.9, f32[1032,128]{1,0:T(8,128)} %bitcast.10, s32[12]{0:T(128)} %old_ref.1, s32[11]{0:T(128)} %new_ref.3, s32[1]{0:T(128)S(6)} %copy.13.lost_ref), custom_call_target="tpu_custom_call" | custom-call | tf_op jit(solution)/shard_map/pallas_call | solution.py:361
  125.7 0.0 copy-done.1
  125.8 0.0 copy-start
  125.8 1.5 %copy-done = f32[16,216,128]{2,1,0:T(8,128)S(1)} copy-done((f32[16,216,128]{2,1,0:T(8,128)S(1)}, f32[16,216,128]{2,1,0:T(8,128)}, u32[]{:S(2)}) %copy-start) | copy-done | bytes 1769496
  127.2 3.0 %shard_map.120 = (f32[1120,128]{1,0:T(8,128)}, f32[1120,128]{1,0:T(8,128)}, f32[1120,128]{1,0:T(8,128)}, bf16[1120,128]{1,0:T(8,128)(2,1)}, f32[4,1120]{1,0:T(4,128)}) custom-call(f32[16,216,128]{2,1,0:T(8,128)S(1)} %copy-done, s32[11]{0:T(128)S(1)} %copy-done.1, s32[1]{0:T(128)S(6)} %copy.13.lost_ref), custom_call_target="tpu_custom_call" | custom-call | tf_op jit(solution)/shard_map/pallas_call | solution.py:412
Async XLA Ops:
  0.6 125.1 %copy-start.1 = (s32[11]{0:T(128)S(1)}, s32[11]{0:T(128)}, u32[]{:S(2)}) copy-start(s32[11]{0:T(128)} %new_ref.3) | copy-start | bytes 136
  125.8 1.5 %copy-start = (f32[16,216,128]{2,1,0:T(8,128)S(1)}, f32[16,216,128]{2,1,0:T(8,128)}, u32[]{:S(2)}) copy-start(f32[16,216,128]{2,1,0:T(8,128)} %shard_map.119.land) | copy-start | bytes 5308420

commit v2 on v1

--- a/solution.py
+++ b/solution.py
@@ -32,8 +32,25 @@
 FEATURE_BLOCK = 512
 F32 = jnp.float32
 
-STREAMS = ((1, 0, 4), (-1, 1, 4), (1, 1, 3), (-1, 0, 3))
-STREAM_BASE = (0, 4, 8, 11)
+STREAMS = ((1, 0, 4), (-1, 0, 3), (-1, 1, 4), (1, 1, 3))
+STREAM_BASE = (0, 4, 7, 11)
+FIRST, SECOND, MASTER = 0, 1, 2
+OLD_PARTS = ((0, 72), (72, 64), (136, 64))
+PART_NEW = SLOT_NEW // 3
+PART_1_AFTER = 3
+LATE = 7
+FAR_FIRST = (8, 9, 7, 10, 6, 11, 5, 12, 4, 13, 3, 14, 2, 15, 1)
+SPANS = 4
+
+
+def groups_near(span):
+    rows = FEATURES // SPANS
+    low, high = span * rows, (span + 1) * rows
+    return [
+        i
+        for i in range(OLD_GROUPS)
+        if max(i, FEATURES - CAP_OLD * (OLD_GROUPS - i)) < high and CAP_OLD * (i + 1) > low
+    ]
 
 
 def prefix(ref, count):
@@ -58,7 +75,7 @@
 def exchange(
     act_hbm, cot_ref, master_hbm, first_hbm, second_hbm, old_ref, new_ref, lost_ref,
     out_hbm,
-    act, cot_t, prod, state, send_old, land_old, sib_send, sib_land, ring_send, ring_land,
+    act, cot_t, prod, state_0, state_1, state_2, send_old, land_old, held_old, sib_send, sib_land, ring_send, ring_land,
     grads, squares, squares_dp, squares_tensor, middle, send_new, starts,
     act_sem, state_sem, local_sem, old_ssem, old_rsem, sib_ssem, sib_rsem, ring_ssem, ring_rsem,
     sq_ssem, sq_rsem, new_ssem, new_rsem,
@@ -85,9 +102,10 @@
             barrier, inc=1, device_id=(dp, lax.rem(tensor + d, DP)), device_id_type=MESH
         )
 
+    state = (state_0, state_1, state_2)
     state_in = [
-        pltpu.make_async_copy(src, state.at[a, pl.ds(16, CAP_OLD)], state_sem.at[a])
-        for a, src in enumerate((master_hbm, first_hbm, second_hbm))
+        pltpu.make_async_copy(src, state[a].at[pl.ds(16, CAP_OLD)], state_sem.at[a])
+        for a, src in ((FIRST, first_hbm), (SECOND, second_hbm), (MASTER, master_hbm))
     ]
     for copy in state_in:
         copy.start()
@@ -109,41 +127,57 @@
         g = jnp.clip(new_group(jnp.int32(h), lost), 0, NEW_GROUPS - 1)
         starts[(h + DP // 2) % DP] = pick(g, new_start)
 
-    for copy in state_in:
-        copy.wait()
+    sends_old = dp <= OLD_GROUPS
+    old_copies = {}
+    for d in range(1, DP):
+        for p, (at, size) in enumerate(OLD_PARTS):
+            old_copies[d, p] = remote(
+                send_old.at[d, pl.ds(at, size)],
+                land_old.at[pl.ds(dp * LAND + 8 + at, size)],
+                old_ssem.at[p, d], old_rsem.at[p, d], lax.rem(dp + d, DP),
+            )
+
+    def pack_old(a):
+        for d in FAR_FIRST:
+            send_old[d, pl.ds(a * OLD_BLOCKS, OLD_BLOCKS), :] = state[a][
+                pl.ds(shift + lax.rem(dp + d, DP), OLD_BLOCKS, stride=16), :
+            ]
+        land_old[pl.ds(dp * LAND + 8 + a * OLD_BLOCKS, OLD_BLOCKS), :] = state[a][
+            pl.ds(shift + dp, OLD_BLOCKS, stride=16), :
+        ]
+
+    def start_old(p, distances=FAR_FIRST):
+        @pl.when(sends_old)
+        def _():
+            for d in distances:
+                old_copies[d, p].start()
+
+    def land_part(p):
+        for d in range(1, DP):
+            @pl.when(lax.rem(dp - d + DP, DP) <= OLD_GROUPS)
+            def _():
+                old_copies[d, p].wait_recv()
+
+        at, size = OLD_PARTS[p]
+        for i in range(OLD_GROUPS + 1):
+            rows = pl.ds(i * LAND + 8 + at, size)
+            held_old[rows, :] = land_old[rows, :]
+
+    def pack_when(a):
+        state_in[a].wait()
+
+        @pl.when(sends_old)
+        def _():
+            pack_old(a)
+
+    pack_when(FIRST)
+    pack_when(SECOND)
     pl.semaphore_wait(barrier, 2 * (DP - 1))
-
-    def pack_old(dst, put):
-        for a in range(3):
-            put(a, state[a, pl.ds(shift + dst, OLD_BLOCKS, stride=16), :])
-
-    old_copies = []
-    for d in range(1, DP):
-        dst = lax.rem(dp + d, DP)
-        old_copies.append(
-            remote(
-                send_old.at[d], land_old.at[pl.ds(dp * LAND + 8, SLOT_OLD)],
-                old_ssem.at[d], old_rsem.at[d], dst,
-            )
-        )
-
-    @pl.when(dp <= OLD_GROUPS)
-    def _():
-        for d in (8, 9, 7, 10, 6, 11, 5, 12, 4, 13, 3, 14, 2, 15, 1):
-            def put(a, rows):
-                send_old[d, pl.ds(a * OLD_BLOCKS, OLD_BLOCKS), :] = rows
-
-            pack_old(lax.rem(dp + d, DP), put)
-            old_copies[d - 1].start()
-
-        def put_own(a, rows):
-            land_old[pl.ds(dp * LAND + 8 + a * OLD_BLOCKS, OLD_BLOCKS), :] = rows
-
-        pack_old(dp, put_own)
+    start_old(0)
 
     cot_t[...] = cot_ref[...].T
-    for b in range(blocks):
-        act_in[b].wait()
+    sibling = dp + 1 - 2 * core
+    sib_copies = {}
 
     def multiply(b, carry):
         columns = pl.ds(pl.multiple_of(b * FEATURE_BLOCK, FEATURE_BLOCK), FEATURE_BLOCK)
@@ -151,28 +185,33 @@
         prod[columns, :] = turned.T
         return carry
 
-    lax.fori_loop(0, blocks, multiply, 0)
-
-    sibling = dp + 1 - 2 * core
-    sib_copies = {}
-    for off in (4, 3, 5, 2, 6, 1, 7, 0):
-        c = lax.rem(chip + off, CHIPS) * 2 + 1 - core
-        sib_send[off] = prod[pl.ds(c, MID, stride=16), :]
-        sib_copies[off] = remote(
-            sib_send.at[off], sib_land.at[off], sib_ssem.at[off], sib_rsem.at[off], sibling
-        )
-        sib_copies[off].start()
+    def chunk(off, half, which):
+        c = lax.rem(chip + off, CHIPS) * 2 + which
+        return prod[pl.ds(c + 16 * HALF * half, HALF, stride=16), :]
+
+    for half in range(2):
+        for b in range(blocks // 2 * half, blocks // 2 * (half + 1)):
+            act_in[b].wait()
+        lax.fori_loop(blocks // 2 * half, blocks // 2 * (half + 1), multiply, 0)
+        for off in (4, 3, 5, 2, 6, 1, 7, 0):
+            sib_send[half, off] = chunk(off, half, 1 - core)
+            copy = remote(
+                sib_send.at[half, off], sib_land.at[half, off],
+                sib_ssem.at[half, off], sib_rsem.at[half, off], sibling,
+            )
+            copy.start()
+            sib_copies[off, half] = copy
+
+    pack_when(MASTER)
 
     arrived = set()
 
     def partial(off, half):
         off = off % CHIPS
-        if off not in arrived:
-            sib_copies[off].wait_recv()
-            arrived.add(off)
-        c = lax.rem(chip + off, CHIPS) * 2 + core
-        own = prod[pl.ds(c + 16 * HALF * half, HALF, stride=16), :]
-        return own + sib_land[off, pl.ds(HALF * half, HALF), :]
+        if (off, half) not in arrived:
+            sib_copies[off, half].wait_recv()
+            arrived.add((off, half))
+        return chunk(off, half, core) + sib_land[half, off]
 
     ring_copies = {}
     for k in range(1, 5):
@@ -190,14 +229,15 @@
                 ring_send.at[n], ring_land.at[n], ring_ssem.at[n], ring_rsem.at[n], neighbour
             )
             ring_copies[n].start()
+        if k == PART_1_AFTER:
+            start_old(1)
     ends = [STREAM_BASE[s] + STREAMS[s][2] - 1 for s in range(4)]
-    for n in ends:
-        ring_copies[n].wait_recv()
     square = jnp.zeros((8, 128), F32)
     for half in range(2):
         total = partial(0, half)
         for s in range(4):
             if STREAMS[s][1] == half:
+                ring_copies[ends[s]].wait_recv()
                 total = total + ring_land[ends[s]]
         grads[pl.ds(HALF * half, HALF), :] = total
         square = square + jnp.sum((total * total).reshape(HALF // 8, 8, 128), axis=0)
@@ -215,96 +255,126 @@
             copies[-1].start()
         return copies
 
+    slots = [jnp.where(lost == i, OLD_GROUPS, i) * LAND + 8 for i in range(OLD_GROUPS)]
+    old_block = [lax.div(s, 16) for s in old_start]
+    old_end = [old_start[i] + old_ref[i] for i in range(OLD_GROUPS)]
+    tiles = MID // 8
+
+    def placed(base, a, near):
+        row = 16 * (base + lax.broadcasted_iota(jnp.int32, (8, 128), 0)) + dp
+        value = jnp.zeros((8, 128), F32)
+        for i in near:
+            live = (row >= old_start[i]) & (row < old_end[i])
+            at = slots[i] + jnp.clip(base - old_block[i], -8, OLD_BLOCKS)
+            value = jnp.where(live, held_old[pl.ds(at + a * OLD_BLOCKS, 8), :], value)
+        return value
+
+    def each_tile(body):
+        for span in range(SPANS):
+            near = groups_near(span)
+
+            def step(m, carry):
+                body(pl.multiple_of(m * 8, 8), near)
+                return carry
+
+            lax.fori_loop(tiles // SPANS * span, tiles // SPANS * (span + 1), step, 0)
+
+    def settle(a):
+        def body(base, near):
+            middle[a, pl.ds(base, 8), :] = placed(base, a, near)
+
+        each_tile(body)
+
     squares[0] = square
     first_gather = gather(squares.at[0], squares_dp, 0, True)
-    for copy in first_gather:
-        copy.wait_recv()
+    start_old(2, FAR_FIRST[:LATE])
+    land_part(0)
+    settle(FIRST)
     for d in range(1, DP):
+        first_gather[d - 1].wait_recv()
         square = square + squares_dp[d]
     squares[1] = square
     second_gather = gather(squares.at[1], squares_tensor, DP, False)
-    for copy in second_gather:
-        copy.wait_recv()
+    start_old(2, FAR_FIRST[LATE:])
+    land_part(1)
+    settle(SECOND)
     for d in range(1, DP):
+        second_gather[d - 1].wait_recv()
         square = square + squares_tensor[d]
     total = jnp.sum(jnp.sum(square, axis=1, keepdims=True), axis=0, keepdims=True)
     count_all = float(FEATURES * 128 * DP)
     clip = 1.0 / jnp.maximum(jnp.sqrt(total / count_all), 1.0)
 
-    for d in range(1, DP):
-        @pl.when(lax.rem(dp - d + DP, DP) <= OLD_GROUPS)
-        def _():
-            old_copies[d - 1].wait_recv()
+    def holds(device):
+        return (device >= DP // 2) | (device < DP // 2 + OLD_GROUPS - DP)
+
+    new_copies = {}
+    for d in range(DP):
+        for a in range(3):
+            part = pl.ds(a * PART_NEW, PART_NEW)
+            if d:
+                new_copies[d, a] = remote(
+                    send_new.at[d, part], out_hbm.at[dp, part],
+                    new_ssem.at[a, d], new_rsem.at[a, d], lax.rem(dp + d, DP),
+                )
+            else:
+                new_copies[d, a] = pltpu.make_async_copy(
+                    send_new.at[0, part], out_hbm.at[dp, part], local_sem.at[a]
+                )
+
+    def start_new(arrays):
+        for d in FAR_FIRST + (0,):
+            dst = lax.rem(dp + d, DP)
+
+            @pl.when(holds(dst))
+            def _():
+                at = lax.div(starts[dst], 16)
+                for a in arrays:
+                    send_new[d, pl.ds(a * PART_NEW, NEW_BLOCKS), :] = middle[
+                        a, pl.ds(at, NEW_BLOCKS), :
+                    ]
+                    new_copies[d, a].start()
+
+    grads[...] = clip * grads[...]
+    g = grads[...]
+    middle[FIRST, pl.ds(0, MID), :] = (
+        beta_first * middle[FIRST, pl.ds(0, MID), :] + (1.0 - beta_first) * g
+    )
+    start_new((FIRST,))
+    middle[SECOND, pl.ds(0, MID), :] = (
+        beta_second * middle[SECOND, pl.ds(0, MID), :] + (1.0 - beta_second) * g * g
+    )
+    start_new((SECOND,))
 
     correct_first = 1.0 - beta_first**10
     correct_second = 1.0 - beta_second**10
-    slots = [jnp.where(lost == i, OLD_GROUPS, i) * LAND + 8 for i in range(OLD_GROUPS)]
-    old_block = [lax.div(s, 16) for s in old_start]
-    old_end = [old_start[i] + old_ref[i] for i in range(OLD_GROUPS)]
-
-    def update(m, carry):
-        base = pl.multiple_of(m * 8, 8)
-        row = 16 * (base + lax.broadcasted_iota(jnp.int32, (8, 128), 0)) + dp
-        values = [jnp.zeros((8, 128), F32) for _ in range(3)]
-        for i in range(OLD_GROUPS):
-            live = (row >= old_start[i]) & (row < old_end[i])
-            at = slots[i] + jnp.clip(base - old_block[i], -8, OLD_BLOCKS)
-            for a in range(3):
-                rows = land_old[pl.ds(at + a * OLD_BLOCKS, 8), :]
-                values[a] = jnp.where(live, rows, values[a])
-        master, first, second = values
-        g = clip * grads[pl.ds(base, 8), :]
-        first = beta_first * first + (1.0 - beta_first) * g
-        second = beta_second * second + (1.0 - beta_second) * g * g
-        master = master - learn_rate * (first / correct_first) / (
-            jnp.sqrt(second / correct_second) + epsilon
-        )
-        middle[0, pl.ds(base, 8), :] = master
-        middle[1, pl.ds(base, 8), :] = first
-        middle[2, pl.ds(base, 8), :] = second
-        return carry
-
-    lax.fori_loop(0, MID // 8, update, 0)
-
-    def holds(device):
-        return (device >= DP // 2) | (device < DP // 2 + OLD_GROUPS - DP)
-
-    new_copies = []
-    for d in range(DP):
-        dst = lax.rem(dp + d, DP)
-        if d:
-            copy = remote(
-                send_new.at[d], out_hbm.at[dp], new_ssem.at[d], new_rsem.at[d], dst
-            )
-        else:
-            copy = pltpu.make_async_copy(send_new.at[0], out_hbm.at[dp], local_sem)
-        new_copies.append(copy)
-    for d in (8, 9, 7, 10, 6, 11, 5, 12, 4, 13, 3, 14, 2, 15, 1, 0):
-        dst = lax.rem(dp + d, DP)
-
-        @pl.when(holds(dst))
-        def _():
-            at = lax.div(starts[dst], 16)
-            for a in range(3):
-                send_new[d, pl.ds(a * NEW_BLOCKS, NEW_BLOCKS), :] = middle[
-                    a, pl.ds(at, NEW_BLOCKS), :
-                ]
-            new_copies[d].start()
+    land_part(2)
+
+    def step_master(base, near):
+        tile = pl.ds(base, 8)
+        middle[MASTER, tile, :] = placed(base, MASTER, near) - learn_rate * (
+            middle[FIRST, tile, :] / correct_first
+        ) / (jnp.sqrt(middle[SECOND, tile, :] / correct_second) + epsilon)
+
+    each_tile(step_master)
+    start_new((MASTER,))
 
     @pl.when(holds(dp))
     def _():
-        for d in range(1, DP):
-            new_copies[d].wait_recv()
-        new_copies[0].wait()
+        for copy in [new_copies[d, a] for a in range(3) for d in range(1, DP)]:
+            copy.wait_recv()
+        for a in range(3):
+            new_copies[0, a].wait()
 
     for d in range(1, DP):
         @pl.when(holds(lax.rem(dp + d, DP)))
         def _():
-            new_copies[d].wait_send()
-
-    @pl.when(dp <= OLD_GROUPS)
+            for a in range(3):
+                new_copies[d, a].wait_send()
+
+    @pl.when(sends_old)
     def _():
-        for copy in old_copies:
+        for copy in old_copies.values():
             copy.wait_send()
 
     for copy in list(sib_copies.values()) + list(ring_copies.values()):
@@ -327,7 +397,7 @@
     for a in range(3):
         for c in range(DP):
             rows[a, pl.ds(c, NEW_BLOCKS, stride=16), :] = land[
-                c, pl.ds(a * NEW_BLOCKS, NEW_BLOCKS), :
+                c, pl.ds(a * PART_NEW, NEW_BLOCKS), :
             ]
     offset = lax.rem(start, 16)
     step = 128
@@ -337,10 +407,10 @@
         taken = [
             jnp.where(live, rows[a, pl.ds(offset + at, size), :], 0.0) for a in range(3)
         ]
-        master_ref[pl.ds(at, size), :] = taken[0]
-        first_ref[pl.ds(at, size), :] = taken[1]
-        second_ref[pl.ds(at, size), :] = taken[2]
-        turned = taken[0].T
+        first_ref[pl.ds(at, size), :] = taken[FIRST]
+        second_ref[pl.ds(at, size), :] = taken[SECOND]
+        master_ref[pl.ds(at, size), :] = taken[MASTER]
+        turned = taken[MASTER].T
         live_turned = at + lax.broadcasted_iota(jnp.int32, (1, size), 1) < length
         parts = []
         for b in range(4):
@@ -367,11 +437,14 @@
             pltpu.VMEM((TOKENS, FEATURES), jnp.bfloat16),
             pltpu.VMEM((128, TOKENS), jnp.bfloat16),
             pltpu.VMEM((FEATURES, 128), F32),
-            pltpu.VMEM((3, CAP_OLD + 56, 128), F32),
+            pltpu.VMEM((CAP_OLD + 56, 128), F32),
+            pltpu.VMEM((CAP_OLD + 56, 128), F32),
+            pltpu.VMEM((CAP_OLD + 56, 128), F32),
             pltpu.VMEM((DP, SLOT_OLD, 128), F32),
             pltpu.VMEM((DP * LAND, 128), F32),
-            pltpu.VMEM((CHIPS, MID, 128), F32),
-            pltpu.VMEM((CHIPS, MID, 128), F32),
+            pltpu.VMEM((DP * LAND, 128), F32),
+            pltpu.VMEM((2, CHIPS, HALF, 128), F32),
+            pltpu.VMEM((2, CHIPS, HALF, 128), F32),
             pltpu.VMEM((14, HALF, 128), F32),
             pltpu.VMEM((14, HALF, 128), F32),
             pltpu.VMEM((MID, 128), F32),
@@ -383,17 +456,17 @@
             pltpu.SMEM((DP,), jnp.int32),
             dma((FEATURES // FEATURE_BLOCK,)),
             dma((3,)),
-            dma,
-            dma((DP,)),
-            dma((DP,)),
-            dma((CHIPS,)),
-            dma((CHIPS,)),
+            dma((3,)),
+            dma((3, DP)),
+            dma((3, DP)),
+            dma((2, CHIPS)),
+            dma((2, CHIPS)),
             dma((14,)),
             dma((14,)),
             dma((2 * DP,)),
             dma((2 * DP,)),
-            dma((DP,)),
-            dma((DP,)),
+            dma((3, DP)),
+            dma((3, DP)),
         ],
         compiler_params=pltpu.CompilerParams(
             collective_id=0, has_side_effects=True, vmem_limit_bytes=56 * 2**20

time: 130 us -> 117 us (0.900)
  Pallas kernels: 127 us -> 114 us
    pallas_call x1, Pallas kernels: 124 us -> 111 us  [on_device(): pl.pallas_call(exchange, out_shape=jax.ShapeDtypeStruct((DP, SLOT_NEW, 12...]
where the time goes in v2:
time: 117 us; the launch traced here: 116 us
  Pallas kernels  114 us (97%)
  local copies, waits for them, and re-layouts  1.47 us (1%)
  between operations  1.33 us (1%)
    pallas_call x1, Pallas kernels, on_device(): pl.pallas_call(exchange, out_shape=jax.ShapeDtypeStruct((DP, SLOT_NEW, 12...  111 us
    pallas_call x1, Pallas kernels, on_device(): pl.pallas_call(place, out_shape=(wide, wide, wide, jax.ShapeDtypeStruct((...  2.98 us

profile of v2, /device:TPU:1, one launch (start us, length us, event | category | flops | bytes accessed | tf_op | source)
XLA Modules:
  0.0 116.4 jit_solution(17436221176726551925)
XLA Ops:
  0.6 0.0 copy-start.1
  1.3 110.7 %shard_map.119.land = f32[16,216,128]{2,1,0:T(8,128)} custom-call(bf16[512,8192]{1,0:T(8,128)(2,1)} %act_hbm.1, bf16[512,128]{1,0:T(8,128)(2,1)} %cot_ref.1, f32[1032,128]{1,0:T(8,128)} %bitcast.8, f32[1032,128]{1,0:T(8,128)} %bitcast.9, f32[1032,128]{1,0:T(8,128)} %bitcast.10, s32[12]{0:T(128)} %old_ref.1, s32[11]{0:T(128)} %new_ref.3, s32[1]{0:T(128)S(6)} %copy.13.lost_ref), custom_call_target="tpu_custom_call" | custom-call | tf_op jit(solution)/shard_map/pallas_call | solution.py:431
  112.0 0.0 copy-done.1
  112.0 0.0 copy-start
  112.0 1.5 %copy-done = f32[16,216,128]{2,1,0:T(8,128)S(1)} copy-done((f32[16,216,128]{2,1,0:T(8,128)S(1)}, f32[16,216,128]{2,1,0:T(8,128)}, u32[]{:S(2)}) %copy-start) | copy-done | bytes 1769496
  113.5 3.0 %shard_map.120 = (f32[1120,128]{1,0:T(8,128)}, f32[1120,128]{1,0:T(8,128)}, f32[1120,128]{1,0:T(8,128)}, bf16[1120,128]{1,0:T(8,128)(2,1)}, f32[4,1120]{1,0:T(4,128)}) custom-call(f32[16,216,128]{2,1,0:T(8,128)S(1)} %copy-done, s32[11]{0:T(128)S(1)} %copy-done.1, s32[1]{0:T(128)S(6)} %copy.13.lost_ref), custom_call_target="tpu_custom_call" | custom-call | tf_op jit(solution)/shard_map/pallas_call | solution.py:485
Async XLA Ops:
  0.6 111.3 %copy-start.1 = (s32[11]{0:T(128)S(1)}, s32[11]{0:T(128)}, u32[]{:S(2)}) copy-start(s32[11]{0:T(128)} %new_ref.3) | copy-start | bytes 136
  112.0 1.5 %copy-start = (f32[16,216,128]{2,1,0:T(8,128)S(1)}, f32[16,216,128]{2,1,0:T(8,128)}, u32[]{:S(2)}) copy-start(f32[16,216,128]{2,1,0:T(8,128)} %shard_map.119.land) | copy-start | bytes 5308420

commit v3 on v2

--- a/solution.py
+++ b/solution.py
@@ -72,12 +72,25 @@
     return holder - jnp.where(holder > lost, 1, 0)
 
 
+def my_rows(dp, lost, new_start, new_ref):
+    holder = lax.rem(dp + DP // 2, DP)
+    group = jnp.clip(new_group(holder, lost), 0, NEW_GROUPS - 1)
+    held = (holder != lost) & (holder < OLD_GROUPS)
+    length = jnp.where(held, pick(group, [new_ref[i] for i in range(NEW_GROUPS)]), 0)
+    return pick(group, new_start), length
+
+
+def interleave(land, rows):
+    for c in range(DP):
+        rows[pl.ds(c, NEW_BLOCKS, stride=16), :] = land[c, pl.ds(0, NEW_BLOCKS), :]
+
+
 def exchange(
-    act_hbm, cot_ref, master_hbm, first_hbm, second_hbm, old_ref, new_ref, lost_ref,
-    out_hbm,
-    act, cot_t, prod, state_0, state_1, state_2, send_old, land_old, held_old, sib_send, sib_land, ring_send, ring_land,
-    grads, squares, squares_dp, squares_tensor, middle, send_new, starts,
-    act_sem, state_sem, local_sem, old_ssem, old_rsem, sib_ssem, sib_rsem, ring_ssem, ring_rsem,
+    act_hbm, cot_hbm, master_hbm, first_hbm, second_hbm, old_ref, new_ref, lost_ref,
+    first_out, second_out, land_master,
+    act, cot_ref, cot_t, prod, state_0, state_1, state_2, send_old, land_old, held_old, sib_send, sib_land, ring_send, ring_land,
+    grads, squares, squares_dp, squares_tensor, middle, send_new, land_first, land_second, rows, starts,
+    act_sem, cot_sem, state_sem, local_sem, old_ssem, old_rsem, sib_ssem, sib_rsem, ring_ssem, ring_rsem,
     sq_ssem, sq_rsem, new_ssem, new_rsem,
 ):
     dp = lax.axis_index("dp")
@@ -109,6 +122,8 @@
     ]
     for copy in state_in:
         copy.start()
+    cot_in = pltpu.make_async_copy(cot_hbm, cot_ref, cot_sem)
+    cot_in.start()
     blocks = FEATURES // FEATURE_BLOCK
     act_in = []
     for b in range(blocks):
@@ -175,6 +190,7 @@
     pl.semaphore_wait(barrier, 2 * (DP - 1))
     start_old(0)
 
+    cot_in.wait()
     cot_t[...] = cot_ref[...].T
     sibling = dp + 1 - 2 * core
     sib_copies = {}
@@ -310,16 +326,15 @@
 
     new_copies = {}
     for d in range(DP):
-        for a in range(3):
-            part = pl.ds(a * PART_NEW, PART_NEW)
+        for a, land in enumerate((land_first, land_second, land_master)):
             if d:
                 new_copies[d, a] = remote(
-                    send_new.at[d, part], out_hbm.at[dp, part],
+                    send_new.at[d, a], land.at[dp],
                     new_ssem.at[a, d], new_rsem.at[a, d], lax.rem(dp + d, DP),
                 )
             else:
                 new_copies[d, a] = pltpu.make_async_copy(
-                    send_new.at[0, part], out_hbm.at[dp, part], local_sem.at[a]
+                    send_new.at[0, a], land.at[dp], local_sem.at[a]
                 )
 
     def start_new(arrays):
@@ -330,7 +345,7 @@
             def _():
                 at = lax.div(starts[dst], 16)
                 for a in arrays:
-                    send_new[d, pl.ds(a * PART_NEW, NEW_BLOCKS), :] = middle[
+                    send_new[d, a, pl.ds(0, NEW_BLOCKS), :] = middle[
                         a, pl.ds(at, NEW_BLOCKS), :
                     ]
                     new_copies[d, a].start()
@@ -359,12 +374,23 @@
     each_tile(step_master)
     start_new((MASTER,))
 
-    @pl.when(holds(dp))
-    def _():
-        for copy in [new_copies[d, a] for a in range(3) for d in range(1, DP)]:
-            copy.wait_recv()
-        for a in range(3):
+    start, length = my_rows(dp, lost, new_start, new_ref)
+
+    def land_new(a):
+        @pl.when(holds(dp))
+        def _():
+            for d in range(1, DP):
+                new_copies[d, a].wait_recv()
             new_copies[0, a].wait()
+
+    for a, land, out in ((FIRST, land_first, first_out), (SECOND, land_second, second_out)):
+        land_new(a)
+        interleave(land, rows.at[a])
+        for at in range(0, CAP_NEW, 160):
+            live = at + lax.broadcasted_iota(jnp.int32, (160, 128), 0) < length
+            taken = rows[a, pl.ds(lax.rem(start, 16) + at, 160), :]
+            out[pl.ds(at, 160), :] = jnp.where(live, taken, 0.0)
+    land_new(MASTER)
 
     for d in range(1, DP):
         @pl.when(holds(lax.rem(dp + d, DP)))
@@ -384,41 +410,49 @@
 
 
 def place(
-    land, new_ref, lost_ref, master_ref, first_ref, second_ref, values_ref, scales_ref, rows
+    land, first, second, new_ref, lost_ref,
+    master_out, first_out, second_out, values_out, scales_out,
+    rows, master, values, scales, sem, master_sem, values_sem,
 ):
-    dp = lax.axis_index("dp")
-    lost = lost_ref[0]
-    new_start = prefix(new_ref, NEW_GROUPS)
-    holder = lax.rem(dp + DP // 2, DP)
-    group = jnp.clip(new_group(holder, lost), 0, NEW_GROUPS - 1)
-    held = (holder != lost) & (holder < OLD_GROUPS)
-    start = pick(group, new_start)
-    length = jnp.where(held, pick(group, [new_ref[i] for i in range(NEW_GROUPS)]), 0)
-    for a in range(3):
-        for c in range(DP):
-            rows[a, pl.ds(c, NEW_BLOCKS, stride=16), :] = land[
-                c, pl.ds(a * PART_NEW, NEW_BLOCKS), :
-            ]
+    copies = [
+        pltpu.make_async_copy(first, first_out, sem.at[0]),
+        pltpu.make_async_copy(second, second_out, sem.at[1]),
+    ]
+    for copy in copies:
+        copy.start()
+    start, length = my_rows(
+        lax.axis_index("dp"), lost_ref[0], prefix(new_ref, NEW_GROUPS), new_ref
+    )
+    interleave(land, rows)
     offset = lax.rem(start, 16)
     step = 128
-    for at in range(0, CAP_NEW, step):
+    for n, at in enumerate(range(0, CAP_NEW, step)):
         size = min(step, CAP_NEW - at)
+        part = pl.ds(at, size)
         live = at + lax.broadcasted_iota(jnp.int32, (size, 128), 0) < length
-        taken = [
-            jnp.where(live, rows[a, pl.ds(offset + at, size), :], 0.0) for a in range(3)
-        ]
-        first_ref[pl.ds(at, size), :] = taken[FIRST]
-        second_ref[pl.ds(at, size), :] = taken[SECOND]
-        master_ref[pl.ds(at, size), :] = taken[MASTER]
-        turned = taken[MASTER].T
+        taken = jnp.where(live, rows[pl.ds(offset + at, size), :], 0.0)
+        master[part, :] = taken
+        copies.append(
+            pltpu.make_async_copy(master.at[part], master_out.at[part], master_sem.at[n])
+        )
+        copies[-1].start()
+        turned = taken.T
         live_turned = at + lax.broadcasted_iota(jnp.int32, (1, size), 1) < length
         parts = []
         for b in range(4):
             block = turned[32 * b : 32 * b + 32]
             scale = jnp.maximum(jnp.max(jnp.abs(block), axis=0, keepdims=True), scale_floor)
             parts.append(block / scale)
-            scales_ref[pl.ds(b, 1), pl.ds(at, size)] = jnp.where(live_turned, scale, 0.0)
-        values_ref[pl.ds(at, size), :] = jnp.concatenate(parts, axis=0).T.astype(jnp.bfloat16)
+            scales[pl.ds(b, 1), part] = jnp.where(live_turned, scale, 0.0)
+        values[part, :] = jnp.concatenate(parts, axis=0).T.astype(jnp.bfloat16)
+        copies.append(
+            pltpu.make_async_copy(values.at[part], values_out.at[part], values_sem.at[n])
+        )
+        copies[-1].start()
+    copies.append(pltpu.make_async_copy(scales, scales_out, sem.at[2]))
+    copies[-1].start()
+    for copy in copies:
+        copy.wait()
 
 
 def on_device(
@@ -428,13 +462,19 @@
     smem = pl.BlockSpec(memory_space=pltpu.SMEM)
     anywhere = pl.BlockSpec(memory_space=pl.ANY)
     dma = pltpu.SemaphoreType.DMA
-    landed = pl.pallas_call(
+    wide = jax.ShapeDtypeStruct((CAP_NEW, 128), F32)
+    first, second, landed = pl.pallas_call(
         exchange,
-        out_shape=jax.ShapeDtypeStruct((DP, SLOT_NEW, 128), F32),
-        in_specs=[anywhere, vmem, anywhere, anywhere, anywhere, smem, smem, smem],
-        out_specs=anywhere,
+        out_shape=(
+            pltpu.VMEM((CAP_NEW, 128), F32),
+            pltpu.VMEM((CAP_NEW, 128), F32),
+            pltpu.VMEM((DP, PART_NEW, 128), F32),
+        ),
+        in_specs=[anywhere] * 5 + [smem] * 3,
+        out_specs=(vmem,) * 3,
         scratch_shapes=[
             pltpu.VMEM((TOKENS, FEATURES), jnp.bfloat16),
+            pltpu.VMEM((TOKENS, 128), jnp.bfloat16),
             pltpu.VMEM((128, TOKENS), jnp.bfloat16),
             pltpu.VMEM((FEATURES, 128), F32),
             pltpu.VMEM((CAP_OLD + 56, 128), F32),
@@ -452,9 +492,13 @@
             pltpu.VMEM((DP, 8, 128), F32),
             pltpu.VMEM((DP, 8, 128), F32),
             pltpu.VMEM((3, MID + 80, 128), F32),
-            pltpu.VMEM((DP, SLOT_NEW, 128), F32),
+            pltpu.VMEM((DP, 3, PART_NEW, 128), F32),
+            pltpu.VMEM((DP, PART_NEW, 128), F32),
+            pltpu.VMEM((DP, PART_NEW, 128), F32),
+            pltpu.VMEM((2, NEW_BLOCKS * 16 + 16, 128), F32),
             pltpu.SMEM((DP,), jnp.int32),
             dma((FEATURES // FEATURE_BLOCK,)),
+            dma,
             dma((3,)),
             dma((3,)),
             dma((3, DP)),
@@ -481,7 +525,7 @@
         new_lengths,
         failed,
     )
-    wide = jax.ShapeDtypeStruct((CAP_NEW, 128), F32)
+    chunks = -(-CAP_NEW // 128)
     outs = pl.pallas_call(
         place,
         out_shape=(
@@ -491,11 +535,23 @@
             jax.ShapeDtypeStruct((CAP_NEW, 128), jnp.bfloat16),
             jax.ShapeDtypeStruct((4, CAP_NEW), F32),
         ),
-        in_specs=[vmem, smem, smem],
-        out_specs=(vmem,) * 5,
-        scratch_shapes=[pltpu.VMEM((3, NEW_BLOCKS * 16 + 16, 128), F32)],
+        in_specs=[vmem, vmem, vmem, smem, smem],
+        out_specs=(anywhere,) * 5,
+        scratch_shapes=[
+            pltpu.VMEM((NEW_BLOCKS * 16 + 16, 128), F32),
+            pltpu.VMEM((CAP_NEW, 128), F32),
+            pltpu.VMEM((CAP_NEW, 128), jnp.bfloat16),
+            pltpu.VMEM((4, CAP_NEW), F32),
+            dma((3,)),
+            dma((chunks,)),
+            dma((chunks,)),
+        ],
         compiler_params=pltpu.CompilerParams(vmem_limit_bytes=32 * 2**20),
-    )(landed, new_lengths, failed)
+    )(
+        *(pltpu.with_memory_space_constraint(x, pltpu.VMEM) for x in (landed, first, second)),
+        new_lengths,
+        failed,
+    )
     return tuple(out[None, None] for out in outs)
 
 

time: 117 us -> 114 us (0.974)
  local copies, waits for them, and re-layouts: 1.47 us -> 0.01 us
    unnamed x4 -> x2, local copies, waits for them, and re-layouts: 1.47 us -> 0.01 us
where the time goes in v3:
time: 114 us
  Pallas kernels  113 us (99%)
  between operations  1.32 us (1%)
    pallas_call x1, Pallas kernels, on_device(): pl.pallas_call(exchange, out_shape=(pltpu.VMEM((CAP_NEW, 128), F32), pltp...  110 us
    pallas_call x1, Pallas kernels, on_device(): pl.pallas_call(place, out_shape=(wide, wide, wide, jax.ShapeDtypeStruct((...  2.61 us

profile of v3, /device:TPU:1, one launch (start us, length us, event | category | flops | bytes accessed | tf_op | source)
XLA Modules:
  0.0 114.3 jit_solution(7396113588783993430)
XLA Ops:
  0.6 0.0 copy-start
  1.3 110.3 %shard_map.119 = (f32[1120,128]{1,0:T(8,128)S(1)}, f32[1120,128]{1,0:T(8,128)S(1)}, f32[16,72,128]{2,1,0:T(8,128)S(1)}) custom-call(bf16[512,8192]{1,0:T(8,128)(2,1)} %act_hbm.1, bf16[512,128]{1,0:T(8,128)(2,1)} %cot_hbm.1, f32[1032,128]{1,0:T(8,128)} %bitcast.8, f32[1032,128]{1,0:T(8,128)} %bitcast.9, f32[1032,128]{1,0:T(8,128)} %bitcast.10, s32[12]{0:T(128)} %old_ref.1, ...), custom_call_target="tpu_custom_call" | custom-call | tf_op jit(solution)/shard_map/pallas_call | solution.py:466
  111.6 0.0 copy-done
  111.7 2.6 %shard_map.120 = (f32[1120,128]{1,0:T(8,128)}, f32[1120,128]{1,0:T(8,128)}, f32[1120,128]{1,0:T(8,128)}, bf16[1120,128]{1,0:T(8,128)(2,1)}, f32[4,1120]{1,0:T(4,128)}) custom-call(f32[16,72,128]{2,1,0:T(8,128)S(1)} %get-tuple-element.13.land, f32[1120,128]{1,0:T(8,128)S(1)} %get-tuple-element.14.first, f32[1120,128]{1,0:T(8,128)S(1)} %get-tuple-element.15.second, ...), custom_call_target="tpu_custom_call" | custom-call | tf_op jit(solution)/shard_map/pallas_call | solution.py:529
Async XLA Ops:
  0.6 111.0 %copy-start = (s32[11]{0:T(128)S(1)}, s32[11]{0:T(128)}, u32[]{:S(2)}) copy-start(s32[11]{0:T(128)} %new_ref.3) | copy-start | bytes 136

commit v4 on v3

--- a/solution.py
+++ b/solution.py
@@ -80,16 +80,12 @@
     return pick(group, new_start), length
 
 
-def interleave(land, rows):
-    for c in range(DP):
-        rows[pl.ds(c, NEW_BLOCKS, stride=16), :] = land[c, pl.ds(0, NEW_BLOCKS), :]
-
-
 def exchange(
-    act_hbm, cot_hbm, master_hbm, first_hbm, second_hbm, old_ref, new_ref, lost_ref,
-    first_out, second_out, land_master,
+    act_hbm, cot_hbm, master_hbm, first_hbm, second_hbm, old_hbm, new_hbm, lost_hbm,
+    first_out, second_out, rows_master, held_out,
     act, cot_ref, cot_t, prod, state_0, state_1, state_2, send_old, land_old, held_old, sib_send, sib_land, ring_send, ring_land,
-    grads, squares, squares_dp, squares_tensor, middle, send_new, land_first, land_second, rows, starts,
+    grads, squares, squares_dp, squares_tensor, middle, send_new, land_first, land_second, land_master, rows, starts,
+    old_ref, new_ref, lost_ref, table_sem,
     act_sem, cot_sem, state_sem, local_sem, old_ssem, old_rsem, sib_ssem, sib_rsem, ring_ssem, ring_rsem,
     sq_ssem, sq_rsem, new_ssem, new_rsem,
 ):
@@ -97,7 +93,6 @@
     tensor = lax.axis_index("tensor")
     chip = lax.div(dp, 2)
     core = lax.rem(dp, 2)
-    lost = lost_ref[0]
 
     def remote(src, dst, ssem, rsem, to_dp, to_tensor=None):
         return pltpu.make_async_remote_copy(
@@ -107,14 +102,23 @@
         )
 
     barrier = pltpu.get_barrier_semaphore()
-    for d in range(1, DP):
+    for d in FAR_FIRST:
         pl.semaphore_signal(
             barrier, inc=1, device_id=(lax.rem(dp + d, DP), tensor), device_id_type=MESH
         )
+    for d in FAR_FIRST:
         pl.semaphore_signal(
             barrier, inc=1, device_id=(dp, lax.rem(tensor + d, DP)), device_id_type=MESH
         )
 
+    tables = [
+        pltpu.make_async_copy(src, dst, table_sem.at[n])
+        for n, (src, dst) in enumerate(
+            ((old_hbm, old_ref), (new_hbm, new_ref), (lost_hbm, lost_ref))
+        )
+    ]
+    for copy in tables:
+        copy.start()
     state = (state_0, state_1, state_2)
     state_in = [
         pltpu.make_async_copy(src, state[a].at[pl.ds(16, CAP_OLD)], state_sem.at[a])
@@ -133,6 +137,9 @@
         )
         act_in[-1].start()
 
+    for copy in tables:
+        copy.wait()
+    lost = lost_ref[0]
     old_start = prefix(old_ref, OLD_GROUPS)
     new_start = prefix(new_ref, NEW_GROUPS)
     my_group = jnp.where(dp == OLD_GROUPS, lost, dp)
@@ -189,6 +196,7 @@
     pack_when(SECOND)
     pl.semaphore_wait(barrier, 2 * (DP - 1))
     start_old(0)
+    pack_when(MASTER)
 
     cot_in.wait()
     cot_t[...] = cot_ref[...].T
@@ -218,7 +226,6 @@
             copy.start()
             sib_copies[off, half] = copy
 
-    pack_when(MASTER)
 
     arrived = set()
 
@@ -350,8 +357,7 @@
                     ]
                     new_copies[d, a].start()
 
-    grads[...] = clip * grads[...]
-    g = grads[...]
+    g = clip * grads[...]
     middle[FIRST, pl.ds(0, MID), :] = (
         beta_first * middle[FIRST, pl.ds(0, MID), :] + (1.0 - beta_first) * g
     )
@@ -374,45 +380,50 @@
     each_tile(step_master)
     start_new((MASTER,))
 
+    @pl.when(sends_old)
+    def _():
+        for copy in old_copies.values():
+            copy.wait_send()
+
+    for copy in list(sib_copies.values()) + list(ring_copies.values()):
+        copy.wait_send()
+    for copy in first_gather + second_gather:
+        copy.wait_send()
+
     start, length = my_rows(dp, lost, new_start, new_ref)
-
-    def land_new(a):
+    held_out[0] = lax.rem(start, 16)
+    held_out[1] = length
+
+    def land_new(a, land, out):
         @pl.when(holds(dp))
         def _():
-            for d in range(1, DP):
-                new_copies[d, a].wait_recv()
-            new_copies[0, a].wait()
+            for d in (0, 1, 15, 2, 14, 3, 13, 4, 12, 5, 11, 6, 10, 7, 9, 8):
+                if d:
+                    new_copies[d, a].wait_recv()
+                else:
+                    new_copies[0, a].wait()
+                c = lax.rem(dp - d + DP, DP)
+                out[pl.ds(c, NEW_BLOCKS, stride=16), :] = land[c, pl.ds(0, NEW_BLOCKS), :]
 
     for a, land, out in ((FIRST, land_first, first_out), (SECOND, land_second, second_out)):
-        land_new(a)
-        interleave(land, rows.at[a])
+        land_new(a, land, rows.at[a])
         for at in range(0, CAP_NEW, 160):
             live = at + lax.broadcasted_iota(jnp.int32, (160, 128), 0) < length
             taken = rows[a, pl.ds(lax.rem(start, 16) + at, 160), :]
             out[pl.ds(at, 160), :] = jnp.where(live, taken, 0.0)
-    land_new(MASTER)
-
     for d in range(1, DP):
         @pl.when(holds(lax.rem(dp + d, DP)))
         def _():
             for a in range(3):
                 new_copies[d, a].wait_send()
 
-    @pl.when(sends_old)
-    def _():
-        for copy in old_copies.values():
-            copy.wait_send()
-
-    for copy in list(sib_copies.values()) + list(ring_copies.values()):
-        copy.wait_send()
-    for copy in first_gather + second_gather:
-        copy.wait_send()
+    land_new(MASTER, land_master, rows_master)
 
 
 def place(
-    land, first, second, new_ref, lost_ref,
+    rows, first, second, held_ref,
     master_out, first_out, second_out, values_out, scales_out,
-    rows, master, values, scales, sem, master_sem, values_sem,
+    master, values, scales, sem, master_sem, values_sem,
 ):
     copies = [
         pltpu.make_async_copy(first, first_out, sem.at[0]),
@@ -420,11 +431,8 @@
     ]
     for copy in copies:
         copy.start()
-    start, length = my_rows(
-        lax.axis_index("dp"), lost_ref[0], prefix(new_ref, NEW_GROUPS), new_ref
-    )
-    interleave(land, rows)
-    offset = lax.rem(start, 16)
+    offset = held_ref[0]
+    length = held_ref[1]
     step = 128
     for n, at in enumerate(range(0, CAP_NEW, step)):
         size = min(step, CAP_NEW - at)
@@ -463,15 +471,16 @@
     anywhere = pl.BlockSpec(memory_space=pl.ANY)
     dma = pltpu.SemaphoreType.DMA
     wide = jax.ShapeDtypeStruct((CAP_NEW, 128), F32)
-    first, second, landed = pl.pallas_call(
+    first, second, landed, held = pl.pallas_call(
         exchange,
         out_shape=(
             pltpu.VMEM((CAP_NEW, 128), F32),
             pltpu.VMEM((CAP_NEW, 128), F32),
-            pltpu.VMEM((DP, PART_NEW, 128), F32),
+            pltpu.VMEM((NEW_BLOCKS * 16 + 16, 128), F32),
+            pltpu.SMEM((2,), jnp.int32),
         ),
-        in_specs=[anywhere] * 5 + [smem] * 3,
-        out_specs=(vmem,) * 3,
+        in_specs=[anywhere] * 8,
+        out_specs=(vmem, vmem, vmem, smem),
         scratch_shapes=[
             pltpu.VMEM((TOKENS, FEATURES), jnp.bfloat16),
             pltpu.VMEM((TOKENS, 128), jnp.bfloat16),
@@ -495,8 +504,13 @@
             pltpu.VMEM((DP, 3, PART_NEW, 128), F32),
             pltpu.VMEM((DP, PART_NEW, 128), F32),
             pltpu.VMEM((DP, PART_NEW, 128), F32),
+            pltpu.VMEM((DP, PART_NEW, 128), F32),
             pltpu.VMEM((2, NEW_BLOCKS * 16 + 16, 128), F32),
             pltpu.SMEM((DP,), jnp.int32),
+            pltpu.SMEM((OLD_GROUPS,), jnp.int32),
+            pltpu.SMEM((NEW_GROUPS,), jnp.int32),
+            pltpu.SMEM((1,), jnp.int32),
+            dma((3,)),
             dma((FEATURES // FEATURE_BLOCK,)),
             dma,
             dma((3,)),
@@ -535,10 +549,9 @@
             jax.ShapeDtypeStruct((CAP_NEW, 128), jnp.bfloat16),
             jax.ShapeDtypeStruct((4, CAP_NEW), F32),
         ),
-        in_specs=[vmem, vmem, vmem, smem, smem],
+        in_specs=[vmem, vmem, vmem, smem],
         out_specs=(anywhere,) * 5,
         scratch_shapes=[
-            pltpu.VMEM((NEW_BLOCKS * 16 + 16, 128), F32),
             pltpu.VMEM((CAP_NEW, 128), F32),
             pltpu.VMEM((CAP_NEW, 128), jnp.bfloat16),
             pltpu.VMEM((4, CAP_NEW), F32),
@@ -549,8 +562,7 @@
         compiler_params=pltpu.CompilerParams(vmem_limit_bytes=32 * 2**20),
     )(
         *(pltpu.with_memory_space_constraint(x, pltpu.VMEM) for x in (landed, first, second)),
-        new_lengths,
-        failed,
+        pltpu.with_memory_space_constraint(held, pltpu.SMEM),
     )
     return tuple(out[None, None] for out in outs)
 

time: 114 us -> 113 us (level)
  Pallas kernels: 113 us -> 111 us
where the time goes in v4:
time: 113 us
  Pallas kernels  111 us (98%)
  between operations  1.29 us (1%)
    pallas_call x1, Pallas kernels, on_device(): pl.pallas_call(exchange, out_shape=(pltpu.VMEM((CAP_NEW, 128), F32), pltp...  109 us

profile of v4, /device:TPU:1, one launch (start us, length us, event | category | flops | bytes accessed | tf_op | source)
XLA Modules:
  0.0 112.5 jit_solution(2256932429240780956)
XLA Ops:
  1.3 109.5 %shard_map.119 = (f32[1120,128]{1,0:T(8,128)S(1)}, f32[1120,128]{1,0:T(8,128)S(1)}, f32[1152,128]{1,0:T(8,128)S(1)}, s32[2]{0:T(128)S(4)}) custom-call(bf16[512,8192]{1,0:T(8,128)(2,1)} %act_hbm.1, bf16[512,128]{1,0:T(8,128)(2,1)} %cot_hbm.1, f32[1032,128]{1,0:T(8,128)} %bitcast.8, f32[1032,128]{1,0:T(8,128)} %bitcast.9, f32[1032,128]{1,0:T(8,128)} %bitcast.10, ...), custom_call_target="tpu_custom_call" | custom-call | tf_op jit(solution)/shard_map/pallas_call | solution.py:474
  110.8 1.8 %shard_map.120 = (f32[1120,128]{1,0:T(8,128)}, f32[1120,128]{1,0:T(8,128)}, f32[1120,128]{1,0:T(8,128)}, bf16[1120,128]{1,0:T(8,128)(2,1)}, f32[4,1120]{1,0:T(4,128)}) custom-call(f32[1152,128]{1,0:T(8,128)S(1)} %get-tuple-element.14.rows, f32[1120,128]{1,0:T(8,128)S(1)} %get-tuple-element.15.first, f32[1120,128]{1,0:T(8,128)S(1)} %get-tuple-element.16.second, ...), custom_call_target="tpu_custom_call" | custom-call | tf_op jit(solution)/shard_map/pallas_call | solution.py:543

commit v5 on v4

--- a/solution.py
+++ b/solution.py
@@ -485,7 +485,7 @@
             pltpu.VMEM((TOKENS, FEATURES), jnp.bfloat16),
             pltpu.VMEM((TOKENS, 128), jnp.bfloat16),
             pltpu.VMEM((128, TOKENS), jnp.bfloat16),
-            pltpu.VMEM((FEATURES, 128), F32),
+            pltpu.VMEM((FEATURES + 16, 128), F32),
             pltpu.VMEM((CAP_OLD + 56, 128), F32),
             pltpu.VMEM((CAP_OLD + 56, 128), F32),
             pltpu.VMEM((CAP_OLD + 56, 128), F32),

time: 113 us -> 113 us (level)
  no operation moved by 1% of the time
where the time goes in v5:
time: 113 us
  Pallas kernels  111 us (98%)
  between operations  1.29 us (1%)
    pallas_call x1, Pallas kernels, on_device(): pl.pallas_call(exchange, out_shape=(pltpu.VMEM((CAP_NEW, 128), F32), pltp...  109 us

profile of v5, /device:TPU:1, one launch (start us, length us, event | category | flops | bytes accessed | tf_op | source)
XLA Modules:
  0.0 112.5 jit_solution(17988154322994219587)
XLA Ops:
  1.3 109.5 %shard_map.119 = (f32[1120,128]{1,0:T(8,128)S(1)}, f32[1120,128]{1,0:T(8,128)S(1)}, f32[1152,128]{1,0:T(8,128)S(1)}, s32[2]{0:T(128)S(4)}) custom-call(bf16[512,8192]{1,0:T(8,128)(2,1)} %act_hbm.1, bf16[512,128]{1,0:T(8,128)(2,1)} %cot_hbm.1, f32[1032,128]{1,0:T(8,128)} %bitcast.8, f32[1032,128]{1,0:T(8,128)} %bitcast.9, f32[1032,128]{1,0:T(8,128)} %bitcast.10, ...), custom_call_target="tpu_custom_call" | custom-call | tf_op jit(solution)/shard_map/pallas_call | solution.py:474
  110.8 1.8 %shard_map.120 = (f32[1120,128]{1,0:T(8,128)}, f32[1120,128]{1,0:T(8,128)}, f32[1120,128]{1,0:T(8,128)}, bf16[1120,128]{1,0:T(8,128)(2,1)}, f32[4,1120]{1,0:T(4,128)}) custom-call(f32[1152,128]{1,0:T(8,128)S(1)} %get-tuple-element.14.rows, f32[1120,128]{1,0:T(8,128)S(1)} %get-tuple-element.15.first, f32[1120,128]{1,0:T(8,128)S(1)} %get-tuple-element.16.second, ...), custom_call_target="tpu_custom_call" | custom-call | tf_op jit(solution)/shard_map/pallas_call | solution.py:543

commit v6 on v5

--- a/solution.py
+++ b/solution.py
@@ -319,8 +319,6 @@
     squares[1] = square
     second_gather = gather(squares.at[1], squares_tensor, DP, False)
     start_old(2, FAR_FIRST[LATE:])
-    land_part(1)
-    settle(SECOND)
     for d in range(1, DP):
         second_gather[d - 1].wait_recv()
         square = square + squares_tensor[d]
@@ -362,6 +360,8 @@
         beta_first * middle[FIRST, pl.ds(0, MID), :] + (1.0 - beta_first) * g
     )
     start_new((FIRST,))
+    land_part(1)
+    settle(SECOND)
     middle[SECOND, pl.ds(0, MID), :] = (
         beta_second * middle[SECOND, pl.ds(0, MID), :] + (1.0 - beta_second) * g * g
     )

time: 113 us -> 113 us (level)
  no operation moved by 1% of the time
where the time goes in v6:
time: 113 us
  Pallas kernels  111 us (98%)
  between operations  1.29 us (1%)
    pallas_call x1, Pallas kernels, on_device(): pl.pallas_call(exchange, out_shape=(pltpu.VMEM((CAP_NEW, 128), F32), pltp...  109 us

profile of v6, /device:TPU:1, one launch (start us, length us, event | category | flops | bytes accessed | tf_op | source)
XLA Modules:
  0.0 112.5 jit_solution(18245852602716346987)
XLA Ops:
  1.3 109.5 %shard_map.119 = (f32[1120,128]{1,0:T(8,128)S(1)}, f32[1120,128]{1,0:T(8,128)S(1)}, f32[1152,128]{1,0:T(8,128)S(1)}, s32[2]{0:T(128)S(4)}) custom-call(bf16[512,8192]{1,0:T(8,128)(2,1)} %act_hbm.1, bf16[512,128]{1,0:T(8,128)(2,1)} %cot_hbm.1, f32[1032,128]{1,0:T(8,128)} %bitcast.8, f32[1032,128]{1,0:T(8,128)} %bitcast.9, f32[1032,128]{1,0:T(8,128)} %bitcast.10, ...), custom_call_target="tpu_custom_call" | custom-call | tf_op jit(solution)/shard_map/pallas_call | solution.py:474
  110.8 1.8 %shard_map.120 = (f32[1120,128]{1,0:T(8,128)}, f32[1120,128]{1,0:T(8,128)}, f32[1120,128]{1,0:T(8,128)}, bf16[1120,128]{1,0:T(8,128)(2,1)}, f32[4,1120]{1,0:T(4,128)}) custom-call(f32[1152,128]{1,0:T(8,128)S(1)} %get-tuple-element.14.rows, f32[1120,128]{1,0:T(8,128)S(1)} %get-tuple-element.15.first, f32[1120,128]{1,0:T(8,128)S(1)} %get-tuple-element.16.second, ...), custom_call_target="tpu_custom_call" | custom-call | tf_op jit(solution)/shard_map/pallas_call | solution.py:543
